TPU v7x, 32 devices: a whole 2x2x4 slice. The times are simulated.
32 devices in a mesh: grp: 2 (over x), own: 16 (over z, y, core).
Axes of the slice: x: 2, y: 2, z: 4, core: 2. Of those that a mesh axis runs over, the one named last changes fastest.
Arguments:
- amps: bfloat16 [896, 128, 128], P(('grp', 'own')), may hold values from -0.35 to 0.35, as said below
- ints: bfloat16 [896, 128, 128], P(('grp', 'own')), may hold values from -0.5 to 0.5, as said below
- pno_energy: float32 [896, 128], P(('grp', 'own')), may hold values from 0.2 to 2, as said below
- occ_energy: float32 [1000], replicated, may hold values from -1 to -0.2
- pair_occ: int32 [2, 896], P(None, ('grp', 'own')), may hold values from 0 to 999, as said below
- mirror: int32 [896], P(('grp', 'own')), may hold values from 0 to 895, as said below
- edge_src: int32 [1536], P(('grp', 'own')), may hold values from 0 to 895, as said below
- edge_dst: int32 [1536], P('grp'), may hold values from 0 to 895, as said below
- edge_fock: float32 [1536], P(('grp', 'own')), may hold values from -6 to 6
- margin: bfloat16 [1536, 128, 128], P(('grp', 'own')), may hold values from -0.15 to 1.15
Outputs:
- residual: bfloat16 [896, 128, 128], P(('grp', 'own'))
Inputs may be any that keep to these rules, and one draw needn't show every extreme that they name: `pair_occ`: each pair's two indices differ. The pair at mirror[p] has its two indices swapped. mirror is an involution without fixed points; a pair and its mirror lie in the same grp block of pairs but never on the same device; amps and ints of mirror[p] are the transposes of those of p, and pno_energy is equal. Of one device's pairs at most 2 have their mirror on any one other device, and that many do for some device. `edge_src`: every edge of a device has its source pair on that same device. `edge_dst`: an edge's target pair lies in the same group as its source, on another device; of one device's edges at most 4 end on pairs of any one other device, and at most 4 have the mirror of their target pair on any one device (that device itself included); both bounds are reached on some device. `amps`: mirror pairs hold transposed tiles. `ints`: mirror pairs hold transposed tiles. `pno_energy`: mirror pairs hold equal rows.
All inputs are finite; a program needn't handle non-finite values.
Results may differ from a plain program's by a relative error of at most 0.0065.
Values may be sent and summed in bfloat16 or wider, within the bound.
A program may use at most 64 MiB of HBM per device.

v0:
```python
import jax
import jax.numpy as jnp
from jax import lax
from jax.sharding import PartitionSpec as P


def rank_within(targets, buckets):
    onehot = (targets[:, None] == lax.iota(jnp.int32, buckets)[None, :]).astype(jnp.int32)
    running = jnp.cumsum(onehot, axis=0)
    return jnp.sum(onehot * running, axis=1) - 1


def pick_rows(lookup, hit_mask):
    return jnp.sum(jnp.where(hit_mask, lookup[None, :], 0.0), axis=1)


def pack_tiles(tile_set, targets, owners, capacity):
    placed = targets * capacity + rank_within(targets, owners)
    blank_buffer = jnp.zeros((owners * capacity,) + tile_set.shape[1:], tile_set.dtype)
    return blank_buffer.at[placed].set(tile_set)


def arrival_sum(arrived, destination, row_ids, row_total, owners, capacity, my_owner):
    per_sender = destination.shape[0] // owners
    arriving = destination == my_owner
    sender = lax.iota(jnp.int32, owners * per_sender) // per_sender
    counted = (
        jnp.cumsum(arriving.reshape(owners, per_sender).astype(jnp.int32), axis=1).reshape(-1) - 1
    )
    column = sender * capacity + counted
    row_hit = (
        (row_ids[:, None] == lax.iota(jnp.int32, row_total)[None, :]) & arriving[:, None]
    ).astype(jnp.float32)
    column_hit = (column[:, None] == lax.iota(jnp.int32, owners * capacity)[None, :]).astype(
        jnp.float32
    )
    selector = jnp.dot(row_hit.T, column_hit).astype(jnp.bfloat16)
    tile_rows = arrived.shape[1]
    tile_cols = arrived.shape[2]
    summed = jnp.dot(
        selector,
        arrived.reshape(owners * capacity, tile_rows * tile_cols),
        preferred_element_type=jnp.float32,
    )
    return summed.reshape(row_total, tile_rows, tile_cols)


def local(
    amps, ints, pno_energy, occ_energy, pair_occ, mirror, edge_src, edge_dst, edge_fock, margin
):
    owners = lax.axis_size("own")
    my_owner = lax.axis_index("own")
    group_index = lax.axis_index("grp")
    per_device = amps.shape[0]
    pno_rank = amps.shape[1]
    edge_count = edge_src.shape[0]
    occ_count = occ_energy.shape[0]
    mirror_cap = (per_device + owners - 2) // (owners - 1)
    edge_cap = (edge_count + owners - 2) // (owners - 1)
    group_base = group_index * (owners * per_device)
    device_base = group_base + my_owner * per_device
    amp_f32 = amps.astype(jnp.float32)
    int_f32 = ints.astype(jnp.float32)
    pair_energy = jnp.sum((2.0 * int_f32 - jnp.swapaxes(int_f32, 1, 2)) * amp_f32, axis=(1, 2))
    occ_ids = lax.iota(jnp.int32, occ_count)
    first_hit = pair_occ[0][:, None] == occ_ids[None, :]
    second_hit = pair_occ[1][:, None] == occ_ids[None, :]
    partial_value = jnp.sum(jnp.where(first_hit, pair_energy[:, None], 0.0), axis=0)
    source_local = edge_src - device_base
    source_tiles = jnp.take(amps, source_local, axis=0)
    projected = jnp.einsum(
        "eab,ebc->eac", margin, source_tiles, preferred_element_type=jnp.float32
    ).astype(jnp.bfloat16)
    product = jnp.einsum("eab,ecb->eac", projected, margin, preferred_element_type=jnp.float32)
    coupled = (product * edge_fock[:, None, None]).astype(jnp.bfloat16)
    group_dst = edge_dst - group_base
    dst_owner = group_dst // per_device
    dst_slot = group_dst % per_device
    my_dst_owner = lax.dynamic_slice_in_dim(dst_owner, my_owner * edge_count, edge_count)
    mirror_local = mirror - group_base
    mirror_owner = mirror_local // per_device
    mirror_slot = mirror_local % per_device
    slot_ids = lax.iota(jnp.int32, per_device)
    same_owner = mirror_owner[:, None] == mirror_owner[None, :]
    out_rank = jnp.sum(same_owner & (slot_ids[None, :] < slot_ids[:, None]), axis=1)
    in_rank = jnp.sum(same_owner & (mirror_slot[None, :] < mirror_slot[:, None]), axis=1)
    out_place = mirror_owner * mirror_cap + out_rank
    in_place = mirror_owner * mirror_cap + in_rank
    outgoing = pack_tiles(coupled, my_dst_owner, owners, edge_cap)
    arrived = lax.all_to_all(outgoing, "own", split_axis=0, concat_axis=0, tiled=True)
    coupling = arrival_sum(arrived, dst_owner, dst_slot, per_device, owners, edge_cap, my_owner)
    occ_sums = lax.psum(partial_value, ("grp", "own"))
    cepa_shift = 0.5 * (pick_rows(occ_sums, first_hit) + pick_rows(occ_sums, second_hit))
    fock_pair = pick_rows(occ_energy, first_hit) + pick_rows(occ_energy, second_hit)
    diagonal = (
        pno_energy[:, :, None]
        + pno_energy[:, None, :]
        - fock_pair[:, None, None]
        - cepa_shift[:, None, None]
    )
    local_part = 0.5 * int_f32 + diagonal * amp_f32
    half_res = (local_part + coupling).astype(jnp.bfloat16)
    sent_tiles = (
        jnp.zeros((owners * mirror_cap, pno_rank, pno_rank), jnp.bfloat16)
        .at[out_place]
        .set(half_res)
    )
    returned = lax.all_to_all(sent_tiles, "own", split_axis=0, concat_axis=0, tiled=True)
    partner_tiles = jnp.swapaxes(jnp.take(returned, in_place, axis=0), 1, 2)
    return (half_res.astype(jnp.float32) + partner_tiles.astype(jnp.float32)).astype(jnp.bfloat16)


def solution(mesh):
    in_specs = (
        P(("grp", "own"), None, None),
        P(("grp", "own"), None, None),
        P(("grp", "own"), None),
        P(),
        P(None, ("grp", "own")),
        P(("grp", "own")),
        P(("grp", "own")),
        P("grp"),
        P(("grp", "own")),
        P(("grp", "own"), None, None),
    )
    out_specs = P(("grp", "own"), None, None)
    return jax.shard_map(local, mesh=mesh, in_specs=in_specs, out_specs=out_specs, check_vma=False)
```

profile of v0, /device:TPU:0, one launch (start us, length us, event | category | flops | bytes accessed | tf_op | source)
XLA Modules:
  0.0 146.0 jit_solution(17444948169573096465)
XLA Ops:
  0.0 0.0 copy-start
  0.0 0.0 copy-start.8
  0.0 0.8 fusion.33
  0.8 0.1 dynamic_slice.3
  0.9 0.1 fusion.24
  1.0 0.1 reduce_window_sum.23
  1.1 0.2 select_reduce_fusion.5
  1.2 0.1 compare_select_fusion.3
  1.3 0.7 compare_and_fusion.3
  2.0 3.1 %gather_fusion = bf16[48,128,128]{2,1,0:T(8,128)(2,1)} fusion(bf16[28,128,128]{2,1,0:T(8,128)(2,1)} %param.10, s32[1024]{0:T(1024)S(1)} %pad_clamp_fusion.1), kind=kCustom, calls=%fused_computation | custom fusion | bytes 3145920 | tf_op jit(solution)/shard_map/jit(_take)/gather | solution.py:70
  5.1 0.0 copy-done
  5.1 0.0 copy-done.8
  5.1 3.7 %multiply_convert_fusion = bf16[48,128,128]{2,1,0:T(8,128)(2,1)S(1)} fusion(bf16[48,128,128]{2,1,0:T(8,128)(2,1)S(1)} %copy-done, f32[48]{0:T(128)S(1)} %copy-done.8, bf16[48,128,128]{2,1,0:T(8,128)(2,1)} %gather_fusion, pred[48]{0:T(512)(128)(4,1)S(1)} %get-tuple-element.18), kind=kOutput, calls=%fused_computation.4 | convolution fusion | flops 405798912 | bytes 4718832 | tf_op jit(solution)/shard_map/eab,ecb->eac/dot_general | solution.py:74
  8.9 1.8 %broadcast_in_dim.101 = bf16[64,128,128]{2,1,0:T(8,128)(2,1)} broadcast(bf16[]{:T(256)} %constant.102.clone.1), dimensions={} | broadcast | bytes 2097154 | tf_op jit(solution)/shard_map/broadcast_in_dim | solution.py:19
  10.7 6.6 %scatter_fusion = bf16[64,128,128]{2,1,0:T(8,128)(2,1)} fusion(bf16[64,128,128]{2,1,0:T(8,128)(2,1)} %broadcast_in_dim.101, s32[48]{0:T(128)S(1)} %compare_select_fusion.3, bf16[48,128,128]{2,1,0:T(8,128)(2,1)S(1)} %multiply_convert_fusion), kind=kCustom, calls=%fused_computation.2 | custom fusion | bytes 4718784 | tf_op jit(solution)/shard_map/scatter | solution.py:20
  17.3 7.5 %all-to-all-start = ((bf16[64,128,128]{2,1,0:T(8,128)(2,1)}), bf16[64,128,128]{2,1,0:T(8,128)(2,1)}, u32[]{:S(2)}, u32[]{:S(2)}) async-start(bf16[64,128,128]{2,1,0:T(8,128)(2,1)} %scatter_fusion), calls=%async_computation | async-start | bytes 4194304 | tf_op jit(solution)/shard_map/all_to_all | solution.py:90
  24.8 0.0 copy-done.2
  24.9 1.3 copy.39
  26.1 0.1 reshape.68
  26.2 0.2 reduce_window_sum.22
  26.4 0.1 sub.71
  26.5 1.5 copy.37
  28.0 0.0 copy-done.6
  28.0 0.0 copy-start.5
  28.0 0.0 copy-start.7
  28.0 0.0 copy-start.4
  28.0 2.0 %fusion.3 = f32[28]{0:T(128)S(1)} fusion(bf16[28,128,128]{1,2,0:T(8,128)(2,1)} %copy.39, f32[28,128,128]{1,2,0:T(8,128)S(1)} %copy.37, bf16[28,128,128]{2,1,0:T(8,128)(2,1)} %param.11), kind=kLoop, calls=%fused_computation.11 | loop fusion | flops 2752484 | bytes 3670128 | tf_op jit(solution)/shard_map/reduce_sum | solution.py:64
  30.1 0.1 select_reduce_fusion.2
  30.2 64.0 %psum.7 = f32[1000]{0:T(1024)S(1)} all-reduce(f32[1000]{0:T(1024)S(1)} %select_reduce_fusion.2), channel_id=1, replica_groups=mesh['grp'=2,'own'=16] {'grp','own'}, use_global_device_ids=true, to_apply=%region_4.5 | all-reduce | flops 1000 | bytes 8000 | tf_op jit(solution)/shard_map/psum | solution.py:92
  94.2 0.0 copy-done.5
  94.2 0.3 select_reduce_fusion
  94.4 0.0 copy-done.7
  94.5 0.2 convert_reduce_fusion.1
  94.7 0.0 copy-done.4
  94.7 0.0 all-to-all-done
  94.7 4.9 %fusion = f32[28,128,128]{2,0,1:T(8,128)} fusion(s32[768]{0:T(1024)S(1)} %get-tuple-element.25, s32[768]{0:T(1024)S(1)} %get-tuple-element.24, pred[768]{0:T(1024)(128)(4,1)S(1)} %get-tuple-element.16, bf16[8,8,128,128]{3,2,1,0:T(8,128)(2,1)} %bitcast.8), kind=kOutput, calls=%fused_computation.8 | convolution fusion | flops 61566720 | bytes 3939072 | tf_op jit(solution)/shard_map/dot_general | solution.py:40
  99.6 2.9 %copy.43 = f32[28,128,128]{1,2,0:T(8,128)} copy(f32[28,128,128]{2,0,1:T(8,128)} %fusion) | data formatting | bytes 3670016 | tf_op jit(solution)/shard_map/dot_general | solution.py:40
  102.6 0.0 copy-done.3
  102.6 3.1 %fusion.6 = bf16[28,128,128]{1,2,0:T(8,128)(2,1)} fusion(f32[28,128,128]{1,2,0:T(8,128)} %copy.43, bf16[28,128,128]{1,2,0:T(8,128)(2,1)} %copy.39, f32[28,128,128]{1,2,0:T(8,128)S(1)} %copy.37, f32[28]{0:T(128)S(1)} %add_multiply_fusion, f32[28]{0:T(128)S(1)} %add.110, f32[28,128]{1,0:T(8,128)S(1)} %copy-done.3), kind=kLoop, calls=%fused_computation.14 | loop fusion | flops 4128768 | bytes 5519584 | tf_op jit(solution)/shard_map/convert_element_type | solution.py:102
  105.6 1.6 %copy.44 = bf16[28,128,128]{2,1,0:T(8,128)(2,1)S(1)} copy(bf16[28,128,128]{1,2,0:T(8,128)(2,1)} %fusion.6) | data formatting | bytes 1835008 | tf_op jit(solution)/shard_map/convert_element_type | solution.py:102
  107.2 1.2 broadcast_in_dim.107
  108.4 4.6 %scatter_fusion.1 = bf16[32,128,128]{2,1,0:T(8,128)(2,1)} fusion(bf16[32,128,128]{2,1,0:T(8,128)(2,1)} %broadcast_in_dim.107, s32[28]{0:T(128)S(1)} %compare_select_fusion, bf16[28,128,128]{2,1,0:T(8,128)(2,1)S(1)} %copy.44), kind=kCustom, calls=%fused_computation.3 | custom fusion | bytes 2752624 | tf_op jit(solution)/shard_map/scatter | solution.py:106
  113.0 5.5 %all-to-all-start.1 = ((bf16[32,128,128]{2,1,0:T(8,128)(2,1)}), bf16[32,128,128]{2,1,0:T(8,128)(2,1)S(1)}, u32[]{:S(2)}, u32[]{:S(2)}) async-start(bf16[32,128,128]{2,1,0:T(8,128)(2,1)} %scatter_fusion.1), calls=%async_computation.1 | async-start | bytes 2097152 | tf_op jit(solution)/shard_map/all_to_all | solution.py:108
  118.6 22.9 %all-to-all-done.1 = bf16[32,128,128]{2,1,0:T(8,128)(2,1)S(1)} async-done(((bf16[32,128,128]{2,1,0:T(8,128)(2,1)}), bf16[32,128,128]{2,1,0:T(8,128)(2,1)S(1)}, u32[]{:S(2)}, u32[]{:S(2)}) %all-to-all-start.1) | async-done | bytes 1048608 | tf_op jit(solution)/shard_map/all_to_all | solution.py:108
  141.5 1.6 %gather_fusion.1 = bf16[28,128,128]{2,1,0:T(8,128)(2,1)} fusion(bf16[32,128,128]{2,1,0:T(8,128)(2,1)S(1)} %all-to-all-done.1, s32[1024]{0:T(1024)S(1)} %pad_clamp_fusion), kind=kCustom, calls=%fused_computation.1 | custom fusion | bytes 1835120 | tf_op jit(solution)/shard_map/jit(_take)/gather | solution.py:109
  143.1 0.0 copy-done.1
  143.1 1.6 %fusion.7 = bf16[28,128,128]{1,2,0:T(8,128)(2,1)S(1)} fusion(bf16[28,128,128]{1,2,0:T(8,128)(2,1)S(1)} %copy-done.1, bf16[28,128,128]{2,1,0:T(8,128)(2,1)} %gather_fusion.1, pred[28]{0:T(512)(128)(4,1)S(1)} %get-tuple-element.13), kind=kLoop, calls=%fused_computation.16 | loop fusion | flops 2293760 | bytes 2752540 | tf_op jit(solution)/shard_map/convert_element_type | solution.py:110
  144.7 1.3 copy.45
  (14 shorter events, 0.1 us)
Async XLA Ops:
  0.0 5.1 %copy-start = (bf16[48,128,128]{2,1,0:T(8,128)(2,1)S(1)}, bf16[48,128,128]{2,1,0:T(8,128)(2,1)}, u32[]{:S(2)}) copy-start(bf16[48,128,128]{2,1,0:T(8,128)(2,1)} %param.19) | copy-start | bytes 4718596
  0.0 5.1 %copy-start.8 = (f32[48]{0:T(128)S(1)}, f32[48]{0:T(128)}, u32[]{:S(2)}) copy-start(f32[48]{0:T(128)} %param.18) | copy-start | bytes 580
  17.3 7.6 %copy-start.2 = (bf16[28,128,128]{2,1,0:T(8,128)(2,1)S(1)}, bf16[28,128,128]{2,1,0:T(8,128)(2,1)}, u32[]{:S(2)}) copy-start(bf16[28,128,128]{2,1,0:T(8,128)(2,1)} %param.10) | copy-start | bytes 2752516
  17.3 77.4 %all-to-all-start = ((bf16[64,128,128]{2,1,0:T(8,128)(2,1)}), bf16[64,128,128]{2,1,0:T(8,128)(2,1)}, u32[]{:S(2)}, u32[]{:S(2)}) async-start(bf16[64,128,128]{2,1,0:T(8,128)(2,1)} %scatter_fusion), calls=%async_computation | async-start | bytes 4194304 | tf_op jit(solution)/shard_map/all_to_all | solution.py:90
  26.1 1.8 %copy-start.6 = (s32[2,28]{1,0:T(2,128)S(1)}, s32[2,28]{1,0:T(2,128)}, u32[]{:S(2)}) copy-start(s32[2,28]{1,0:T(2,128)} %param.14) | copy-start | bytes 676
  28.0 66.2 %copy-start.5 = (f32[1000]{0:T(1024)S(1)}, f32[1000]{0:T(1024)}, u32[]{:S(2)}) copy-start(f32[1000]{0:T(1024)} %param.13) | copy-start | bytes 12004
  28.0 66.5 %copy-start.7 = (s32[28]{0:T(128)S(1)}, s32[28]{0:T(128)}, u32[]{:S(2)}) copy-start(s32[28]{0:T(128)} %param.15) | copy-start | bytes 340
  28.0 66.7 %copy-start.4 = (s32[768]{0:T(1024)S(1)}, s32[768]{0:T(1024)}, u32[]{:S(2)}) copy-start(s32[768]{0:T(1024)} %param.17) | copy-start | bytes 9220
  99.6 2.9 %copy-start.3 = (f32[28,128]{1,0:T(8,128)S(1)}, f32[28,128]{1,0:T(8,128)}, u32[]{:S(2)}) copy-start(f32[28,128]{1,0:T(8,128)} %param.12) | copy-start | bytes 43012
  113.0 30.1 %copy-start.1 = (bf16[28,128,128]{1,2,0:T(8,128)(2,1)S(1)}, bf16[28,128,128]{1,2,0:T(8,128)(2,1)}, u32[]{:S(2)}) copy-start(bf16[28,128,128]{1,2,0:T(8,128)(2,1)} %fusion.6) | copy-start | bytes 2752516
  113.0 28.5 %all-to-all-start.1 = ((bf16[32,128,128]{2,1,0:T(8,128)(2,1)}), bf16[32,128,128]{2,1,0:T(8,128)(2,1)S(1)}, u32[]{:S(2)}, u32[]{:S(2)}) async-start(bf16[32,128,128]{2,1,0:T(8,128)(2,1)} %scatter_fusion.1), calls=%async_computation.1 | async-start | bytes 2097152 | tf_op jit(solution)/shard_map/all_to_all | solution.py:108
where the time goes:
time: 148 us; the launch traced here: 146 us
  blocking collectives  64 us (43%)
  local copies, waits for them, and re-layouts  27.7 us (19%)
  waiting for transfers between devices  22.9 us (15%)
  starting transfers between devices  13.1 us (9%)
  other arithmetic  9.46 us (6%)
  matrix products  8.62 us (6%)
    psum x1, blocking collectives, local(): occ_sums = lax.psum(partial_value, ('grp', 'own'))  64 us
    all_to_all x1, waiting for transfers between devices, local(): lax.all_to_all(sent_tiles, 'own', split_axis=0, concat_axis=0, tiled=True)  22.9 us
    all_to_all x1, starting transfers between devices, local(): lax.all_to_all(outgoing, 'own', split_axis=0, concat_axis=0, tiled=True)  7.55 us
    scatter x1, local copies, waits for them, and re-layouts, pack_tiles(): return blank_buffer.at[placed].set(tile_set)  6.62 us
    all_to_all x1, starting transfers between devices, local(): lax.all_to_all(sent_tiles, 'own', split_axis=0, concat_axis=0, tiled=True)  5.53 us
    dot_general x1, matrix products, arrival_sum(): jnp.dot(selector, arrived.reshape(owners * capacity, tile_rows * tile_col...  4.9 us
    scatter x1, local copies, waits for them, and re-layouts, local(): sent_tiles = jnp.zeros((owners * mirror_cap, pno_rank, pno_rank), jnp.bfl...  4.55 us
    dot_general x1, matrix products, local(): jnp.einsum('eab,ecb->eac', projected, margin, preferred_element_type=jnp....  3.73 us
  transfers between devices with their start and end apart: 2, of which 1 were waited for; matrix products, arithmetic and copies ran while one was open for 4% of the time, Pallas kernels for 0%

commit v1 on v0

v1 whole, which is shorter than its diff:
```python
import functools

import jax
import jax.numpy as jnp
from jax import lax
from jax.experimental import pallas as pl
from jax.experimental.pallas import tpu as pltpu
from jax.sharding import PartitionSpec as P

MESH = pl.DeviceIdType.MESH
LANES = 128
EARLY_STEPS = 4


def step_offset(step, devices):
    half = (step + 1) // 2
    signed = jnp.where(step % 2 == 1, devices - 1 - half, half)
    return 1 + lax.rem(devices // 2 - 1 + signed, devices - 1)


def kernel(
    dims,
    ids,
    scales,
    amps,
    ints,
    pno,
    margin,
    out,
    send_edge,
    recv_edge,
    running,
    local_part,
    send_half,
    recv_half,
    flipped,
    grp_sums,
    own_sums,
    edge_send_sem,
    edge_recv_sem,
    half_send_sem,
    half_recv_sem,
    grp_send_sem,
    grp_recv_sem,
    own_send_sem,
    own_recv_sem,
):
    groups, owners, pairs, edge_cap, mirror_cap, occ_rows = dims
    edge_slots = owners * edge_cap
    half_slots = owners * mirror_cap
    rank = amps.shape[1]
    group = lax.axis_index("grp")
    me = lax.axis_index("own")

    at_edge, at_src, at_order = 0, edge_slots, 2 * edge_slots
    at_last = 3 * edge_slots
    at_first, at_second = at_last + pairs, at_last + 2 * pairs
    at_pack = at_last + 3 * pairs
    at_in = at_pack + half_slots
    at_out = at_in + pairs
    at_keep, at_has = edge_slots, 2 * edge_slots
    at_fock = at_has + pairs

    barrier = pltpu.get_barrier_semaphore()

    @pl.loop(1, owners)
    def _(offset):
        pl.semaphore_signal(
            barrier,
            inc=1,
            device_id=(group, lax.rem(me + offset, owners)),
            device_id_type=MESH,
        )

    @pl.loop(1, groups)
    def _(offset):
        pl.semaphore_signal(
            barrier,
            inc=1,
            device_id=(lax.rem(group + offset, groups), me),
            device_id_type=MESH,
        )

    pl.semaphore_wait(barrier, owners + groups - 2)

    def edge_copy(offset):
        target = lax.rem(me + offset, owners)
        return pltpu.make_async_remote_copy(
            src_ref=send_edge.at[pl.ds(target * edge_cap, edge_cap)],
            dst_ref=recv_edge.at[pl.ds(me * edge_cap, edge_cap)],
            send_sem=edge_send_sem.at[offset],
            recv_sem=edge_recv_sem.at[offset],
            device_id=(group, target),
            device_id_type=MESH,
        )

    def half_copy(offset):
        target = lax.rem(me + offset, owners)
        return pltpu.make_async_remote_copy(
            src_ref=send_half.at[pl.ds(target * mirror_cap, mirror_cap)],
            dst_ref=recv_half.at[pl.ds(me * mirror_cap, mirror_cap)],
            send_sem=half_send_sem.at[offset],
            recv_sem=half_recv_sem.at[offset],
            device_id=(group, target),
            device_id_type=MESH,
        )

    def grp_copy(offset):
        return pltpu.make_async_remote_copy(
            src_ref=grp_sums.at[group],
            dst_ref=grp_sums.at[group],
            send_sem=grp_send_sem.at[offset],
            recv_sem=grp_recv_sem.at[offset],
            device_id=(lax.rem(group + offset, groups), me),
            device_id_type=MESH,
        )

    def own_copy(offset):
        return pltpu.make_async_remote_copy(
            src_ref=own_sums.at[me],
            dst_ref=own_sums.at[me],
            send_sem=own_send_sem.at[offset],
            recv_sem=own_recv_sem.at[offset],
            device_id=(group, lax.rem(me + offset, owners)),
            device_id_type=MESH,
        )

    def send_step(step):
        offset = step_offset(step, owners)
        target = lax.rem(me + offset, owners)
        for k in range(edge_cap):
            slot = target * edge_cap + k
            tile = margin[ids[at_edge + slot]]
            projected = jnp.dot(
                tile, amps[ids[at_src + slot]], preferred_element_type=jnp.float32
            ).astype(jnp.bfloat16)
            product = lax.dot_general(
                projected, tile, (((1,), (1,)), ((), ())), preferred_element_type=jnp.float32
            )
            send_edge[slot] = (product * scales[slot]).astype(jnp.bfloat16)
        edge_copy(offset).start()

    early = min(EARLY_STEPS, owners - 1)
    pl.loop(0, early)(send_step)

    rows = lax.broadcasted_iota(jnp.int32, (rank, rank), 0)
    columns = lax.broadcasted_iota(jnp.int32, (rank, rank), 1)
    on_diagonal = rows == columns
    occ_ids = lax.broadcasted_iota(
        jnp.int32, (occ_rows, LANES), 0
    ) * LANES + lax.broadcasted_iota(jnp.int32, (occ_rows, LANES), 1)

    def add_energy(p, partial):
        int_tile, amp_tile = ints[p], amps[p]
        product = jnp.dot(int_tile, amp_tile, preferred_element_type=jnp.float32)
        direct = 2.0 * int_tile.astype(jnp.float32) * amp_tile.astype(jnp.float32)
        terms = direct - jnp.where(on_diagonal, product, 0.0)
        energy = jnp.sum(jnp.sum(terms, axis=0, keepdims=True), axis=1, keepdims=True)
        return partial + jnp.where(occ_ids == ids[at_first + p], energy, 0.0)

    partial = lax.fori_loop(0, pairs, add_energy, jnp.zeros((occ_rows, LANES), jnp.float32))
    grp_sums[group] = partial

    @pl.loop(1, groups)
    def _(offset):
        grp_copy(offset).start()

    pl.loop(early, owners - 1)(send_step)

    @pl.loop(1, groups)
    def _(offset):
        grp_copy(offset).wait()

    own_sums[me] = jnp.sum(grp_sums[...], axis=0)

    @pl.loop(1, owners)
    def _(offset):
        own_copy(offset).start()

    for k in range(edge_cap):
        recv_edge[me * edge_cap + k] = jnp.zeros((rank, rank), jnp.bfloat16)

    @pl.loop(1, owners)
    def _(offset):
        own_copy(offset).wait()

    occ_sum = jnp.sum(own_sums[...], axis=0)

    @pl.loop(0, pairs)
    def _(p):
        hits = jnp.where(occ_ids == ids[at_first + p], occ_sum, 0.0) + jnp.where(
            occ_ids == ids[at_second + p], occ_sum, 0.0
        )
        shift = 0.5 * jnp.sum(jnp.sum(hits, axis=0, keepdims=True), axis=1, keepdims=True)
        across = jnp.broadcast_to(pno[p], (rank, rank))
        diagonal = ((across + across.T) - scales[at_fock + p]) - shift
        local_part[p] = 0.5 * ints[p].astype(jnp.float32) + diagonal * amps[p].astype(jnp.float32)

    @pl.loop(1, owners)
    def _(offset):
        edge_copy(offset).wait()

    def accumulate(j, total):
        total = total * scales[at_keep + j] + recv_edge[ids[at_order + j]].astype(jnp.float32)
        running[j] = total
        return total

    lax.fori_loop(0, edge_slots, accumulate, jnp.zeros((rank, rank), jnp.float32))

    @pl.loop(0, owners - 1)
    def _(step):
        offset = step_offset(step, owners)
        target = lax.rem(me + offset, owners)
        for k in range(mirror_cap):
            slot = target * mirror_cap + k
            p = ids[at_pack + slot]
            coupling = running[ids[at_last + p]] * scales[at_has + p]
            send_half[slot] = (local_part[p] + coupling).astype(jnp.bfloat16)
        half_copy(offset).start()

    @pl.loop(0, owners - 1)
    def _(step):
        offset = step_offset(step, owners)
        half_copy(offset).wait_recv()
        sender = lax.rem(me - offset + owners, owners)
        for k in range(mirror_cap):
            slot = sender * mirror_cap + k
            flipped[slot] = recv_half[slot].astype(jnp.float32).T

    @pl.loop(0, pairs)
    def _(p):
        own_tile = send_half[ids[at_out + p]].astype(jnp.float32)
        out[p] = (own_tile + flipped[ids[at_in + p]]).astype(jnp.bfloat16)

    @pl.loop(1, owners)
    def _(offset):
        half_copy(offset).wait_send()


def local(
    amps, ints, pno_energy, occ_energy, pair_occ, mirror, edge_src, edge_dst, edge_fock, margin
):
    groups = lax.axis_size("grp")
    owners = lax.axis_size("own")
    my_owner = lax.axis_index("own")
    group_index = lax.axis_index("grp")
    pairs = amps.shape[0]
    rank = amps.shape[1]
    edge_count = edge_src.shape[0]
    occ_count = occ_energy.shape[0]
    mirror_cap = (pairs + owners - 2) // (owners - 1)
    edge_cap = (edge_count + owners - 2) // (owners - 1)
    edge_slots = owners * edge_cap
    half_slots = owners * mirror_cap
    group_base = group_index * (owners * pairs)
    device_base = group_base + my_owner * pairs
    iota = functools.partial(lax.iota, jnp.int32)

    group_dst = edge_dst - group_base
    dst_owner = group_dst // pairs
    dst_slot = group_dst % pairs
    mine = lax.dynamic_slice_in_dim(dst_owner, my_owner * edge_count, edge_count)
    earlier = iota(edge_count)[None, :] < iota(edge_count)[:, None]
    place = mine * edge_cap + jnp.sum(
        ((mine[:, None] == mine[None, :]) & earlier).astype(jnp.int32), axis=1
    )
    placed = place[None, :] == iota(edge_slots)[:, None]
    slot_edge = jnp.sum(jnp.where(placed, iota(edge_count)[None, :], 0), axis=1)
    slot_src = jnp.sum(jnp.where(placed, (edge_src - device_base)[None, :], 0), axis=1)
    slot_fock = jnp.sum(jnp.where(placed, edge_fock[None, :], 0.0), axis=1)

    owner_rows = dst_owner.reshape(owners, edge_count)
    arriving = owner_rows == my_owner
    rank_rows = jnp.sum(
        (arriving[:, None, :] & earlier[None, :, :]).astype(jnp.int32), axis=2
    )
    here = arriving[:, :, None] & (rank_rows[:, :, None] == iota(edge_cap)[None, None, :])
    slot_rows = dst_slot.reshape(owners, edge_count)[:, :, None] - pairs
    arrived_dst = (jnp.sum(jnp.where(here, slot_rows, 0), axis=1) + pairs).reshape(-1)
    sort_key = arrived_dst * edge_slots + iota(edge_slots)
    position = jnp.sum((sort_key[None, :] < sort_key[:, None]).astype(jnp.int32), axis=1)
    sorted_hit = position[None, :] == iota(edge_slots)[:, None]
    order = jnp.sum(jnp.where(sorted_hit, iota(edge_slots)[None, :], 0), axis=1)
    sorted_dst = jnp.sum(jnp.where(sorted_hit, arrived_dst[None, :], 0), axis=1)
    keep = jnp.concatenate(
        [jnp.zeros((1,), jnp.float32), (sorted_dst[1:] == sorted_dst[:-1]).astype(jnp.float32)]
    )
    pair_ids = iota(pairs)
    up_to = jnp.sum((arrived_dst[None, :] <= pair_ids[:, None]).astype(jnp.int32), axis=1)
    last = jnp.maximum(up_to - 1, 0)
    has = jnp.max((arrived_dst[None, :] == pair_ids[:, None]).astype(jnp.float32), axis=1)

    mirror_local = mirror - group_base
    mirror_owner = mirror_local // pairs
    mirror_slot = mirror_local % pairs
    same_owner = mirror_owner[:, None] == mirror_owner[None, :]
    out_rank = jnp.sum(
        (same_owner & (pair_ids[None, :] < pair_ids[:, None])).astype(jnp.int32), axis=1
    )
    in_rank = jnp.sum(
        (same_owner & (mirror_slot[None, :] < mirror_slot[:, None])).astype(jnp.int32), axis=1
    )
    out_place = mirror_owner * mirror_cap + out_rank
    in_place = mirror_owner * mirror_cap + in_rank
    pack = jnp.sum(
        jnp.where(out_place[None, :] == iota(half_slots)[:, None], pair_ids[None, :], 0), axis=1
    )

    occ_ids = iota(occ_count)
    occ_hit = (pair_occ[0][:, None] == occ_ids[None, :]).astype(jnp.float32) + (
        pair_occ[1][:, None] == occ_ids[None, :]
    ).astype(jnp.float32)
    fock_pair = jnp.sum(occ_hit * occ_energy[None, :], axis=1)

    ids = jnp.concatenate(
        [slot_edge, slot_src, order, last, pair_occ[0], pair_occ[1], pack, in_place, out_place]
    )
    scales = jnp.concatenate([slot_fock, keep, has, fock_pair])

    occ_rows = -(-occ_count // LANES)
    dims = (groups, owners, pairs, edge_cap, mirror_cap, occ_rows)
    vmem = pl.BlockSpec(memory_space=pltpu.VMEM)
    smem = pl.BlockSpec(memory_space=pltpu.SMEM)
    dma = pltpu.SemaphoreType.DMA
    return pl.pallas_call(
        functools.partial(kernel, dims),
        out_shape=jax.ShapeDtypeStruct(amps.shape, jnp.bfloat16),
        in_specs=[smem, smem, vmem, vmem, vmem, vmem],
        out_specs=vmem,
        scratch_shapes=[
            pltpu.VMEM((edge_slots, rank, rank), jnp.bfloat16),
            pltpu.VMEM((edge_slots, rank, rank), jnp.bfloat16),
            pltpu.VMEM((edge_slots, rank, rank), jnp.float32),
            pltpu.VMEM((pairs, rank, rank), jnp.float32),
            pltpu.VMEM((half_slots, rank, rank), jnp.bfloat16),
            pltpu.VMEM((half_slots, rank, rank), jnp.bfloat16),
            pltpu.VMEM((half_slots, rank, rank), jnp.float32),
            pltpu.VMEM((groups, occ_rows, LANES), jnp.float32),
            pltpu.VMEM((owners, occ_rows, LANES), jnp.float32),
            dma((owners,)),
            dma((owners,)),
            dma((owners,)),
            dma((owners,)),
            dma((groups,)),
            dma((groups,)),
            dma((owners,)),
            dma((owners,)),
        ],
        compiler_params=pltpu.CompilerParams(
            collective_id=0, has_side_effects=True, vmem_limit_bytes=56 * 1024 * 1024
        ),
    )(ids, scales, amps, ints, pno_energy.reshape(pairs, 1, rank), margin)


def solution(mesh):
    in_specs = (
        P(("grp", "own"), None, None),
        P(("grp", "own"), None, None),
        P(("grp", "own"), None),
        P(),
        P(None, ("grp", "own")),
        P(("grp", "own")),
        P(("grp", "own")),
        P("grp"),
        P(("grp", "own")),
        P(("grp", "own"), None, None),
    )
    out_specs = P(("grp", "own"), None, None)
    return jax.shard_map(local, mesh=mesh, in_specs=in_specs, out_specs=out_specs, check_vma=False)
```

time: 148 us -> 99.8 us (0.67); the launches traced: 146 us -> 99.5 us
  Pallas kernels: 0 us -> 87.2 us
  blocking collectives: 64 us -> 0 us
  waiting for transfers between devices: 22.9 us -> 0 us
  local copies, waits for them, and re-layouts: 27.7 us -> 6.06 us
  starting transfers between devices: 13.1 us -> 0 us
  matrix products: 8.62 us -> 0 us
  other arithmetic: 9.46 us -> 6.16 us
    pallas_call x0 -> x1, Pallas kernels: none -> 87.2 us  [local(): pl.pallas_call(functools.partial(kernel, dims), out_shape=jax.ShapeDtypeS...]
    psum x1 -> x0, blocking collectives: 64 us -> none  [local(): occ_sums = lax.psum(partial_value, ('grp', 'own'))]
    all_to_all x2 -> x0, waiting for transfers between devices: 22.9 us -> none  [the longest x1 22.9 us: local(): lax.all_to_all(sent_tiles, 'own', split_axis=0, concat_axis=0, tiled=True)]
    all_to_all x2 -> x0, starting transfers between devices: 13.1 us -> none  [the longest x1 7.55 us: local(): lax.all_to_all(outgoing, 'own', split_axis=0, concat_axis=0, tiled=True)]
    scatter x2 -> x0, local copies, waits for them, and re-layouts: 11.2 us -> none  [the longest x1 6.62 us: pack_tiles(): return blank_buffer.at[placed].set(tile_set)]
    dot_general x2 -> x0, matrix products: 8.62 us -> none  [the longest x1 4.9 us: arrival_sum(): jnp.dot(selector, arrived.reshape(owners * capacity, tile_rows * tile_col...]
    convert_element_type x4 -> x1, other arithmetic: 5.59 us -> 0.07 us  [local(): (sorted_dst[1:] == sorted_dst[:-1]).astype(jnp.float32)]
    gather x2 -> x0, local copies, waits for them, and re-layouts: 4.74 us -> none  [the longest x1 3.13 us: local(): source_tiles = jnp.take(amps, source_local, axis=0)]
  transfers between devices with their start and end apart: 2 -> 0, of which waited for: 1 -> 0; matrix products, arithmetic and copies ran while one was open for 4% -> 0% of each run, Pallas kernels for 0% -> 0%
where the time goes in v1:
time: 99.8 us; the launch traced here: 99.5 us
  Pallas kernels  87.2 us (87%)
  other arithmetic  6.16 us (6%)
  local copies, waits for them, and re-layouts  6.06 us (6%)
    pallas_call x1, Pallas kernels, local(): pl.pallas_call(functools.partial(kernel, dims), out_shape=jax.ShapeDtypeS...  87.2 us
    unnamed x1, local copies, waits for them, and re-layouts  2.2 us

profile of v1, /device:TPU:0, one launch (start us, length us, event | category | flops | bytes accessed | tf_op | source)
XLA Modules:
  0.0 99.5 jit_solution(12072538592780025342)
XLA Ops:
  0.0 0.8 slice_bitcast_fusion
  0.8 0.9 multiply_reduce_fusion
  1.6 0.7 and_select_fusion.1
  2.3 0.2 convert_reduce_fusion.4
  2.5 0.7 fusion.1
  3.2 0.1 sub.43
  3.3 0.7 broadcast_compare_fusion
  4.0 0.1 dynamic_slice.3
  4.1 0.2 convert_reduce_fusion.2
  4.3 0.7 multiply_add_fusion
  5.0 0.7 select_reduce_fusion.3
  5.8 0.1 select_reduce_fusion.4
  5.8 0.1 eq.145
  6.0 0.4 convert_reduce_fusion
  6.3 0.1 select_reduce_fusion.2
  6.5 0.1 copy.11
  6.6 0.1 add.78
  6.7 0.1 convert_reduce_fusion.3
  6.8 0.1 convert_reduce_fusion.6
  6.9 0.1 select_reduce_fusion.6
  7.0 0.2 convert_reduce_fusion.1
  7.2 0.1 select_reduce_fusion
  7.3 0.7 concatenate.6.ids
  8.0 0.1 compare_convert_fusion
  8.1 0.7 concatenate.7.scales
  8.8 1.3 %reshape.79.pno = f32[28,1,128]{2,1,0:T(1,128)} reshape(f32[28,128]{1,0:T(8,128)} %param.12) | data formatting | bytes 28672 | tf_op jit(solution)/shard_map/reshape | solution.py:352
  10.1 87.2 %shard_map.100 = bf16[28,128,128]{2,1,0:T(8,128)(2,1)} custom-call(s32[364]{0:T(512)} %concatenate.6.ids, f32[184]{0:T(256)} %concatenate.7.scales, bf16[28,128,128]{2,1,0:T(8,128)(2,1)} %amps.1, bf16[28,128,128]{2,1,0:T(8,128)(2,1)} %ints.1, f32[28,1,128]{2,1,0:T(1,128)} %reshape.79.pno, bf16[48,128,128]{2,1,0:T(8,128)(2,1)} %margin.1), custom_call_target="tpu_custom_call" | custom-call | tf_op jit(solution)/shard_map/pallas_call | solution.py:325
  97.3 2.2 %copy.13 = bf16[28,128,128]{2,1,0:T(8,128)(2,1)} copy(bf16[28,128,128]{2,1,0:T(8,128)(2,1)} %shard_map.100) | data formatting | bytes 1835008
  (4 shorter events, 0.0 us)

commit v2 on v1

v2 whole, which is shorter than its diff:
```python
import functools

import jax
import jax.numpy as jnp
from jax import lax
from jax.experimental import pallas as pl
from jax.experimental.pallas import tpu as pltpu
from jax.sharding import PartitionSpec as P

MESH = pl.DeviceIdType.MESH
LANES = 128
EARLY_STEPS = 4


def step_offset(step, devices):
    spread = jnp.where(step % 2 == 1, devices - 2 - step // 2, step // 2)
    half = (spread + 1) // 2
    signed = jnp.where(spread % 2 == 1, devices - 1 - half, half)
    return 1 + lax.rem(devices // 2 - 1 + signed, devices - 1)


def within(index, size):
    return jnp.minimum(jnp.maximum(index, 0), size - 1)


def kernel(
    dims,
    occ,
    occ_energy,
    mirror,
    edge_src,
    edge_dst,
    edge_fock,
    pno,
    amps,
    ints,
    margin,
    out,
    send_edge,
    recv_edge,
    running,
    local_part,
    send_half,
    recv_half,
    flipped,
    grp_sums,
    own_sums,
    table,
    early_rows,
    early_scale_rows,
    late_rows,
    late_scale_rows,
    early,
    early_scales,
    late,
    late_scales,
    table_sem,
    edge_send_sem,
    edge_recv_sem,
    half_send_sem,
    half_recv_sem,
    grp_send_sem,
    grp_recv_sem,
    own_send_sem,
    own_recv_sem,
):
    groups, owners, pairs, edge_cap, mirror_cap, occ_rows = dims
    edge_slots = owners * edge_cap
    half_slots = owners * mirror_cap
    rank = amps.shape[1]
    group = lax.axis_index("grp")
    me = lax.axis_index("own")

    width = table.shape[1]
    at_slot, at_src, at_fock = owners, 2 * owners, 2 * owners + 1
    at_partner, at_place = 2 * owners + 2, 2 * owners + 3
    at_occ = 2 * owners + 4
    edge_count = edge_src.shape[1]
    occ_count = occ_energy.shape[1]

    barrier = pltpu.get_barrier_semaphore()

    @pl.loop(1, owners)
    def _(offset):
        pl.semaphore_signal(
            barrier,
            inc=1,
            device_id=(group, lax.rem(me + offset, owners)),
            device_id_type=MESH,
        )

    @pl.loop(1, groups)
    def _(offset):
        pl.semaphore_signal(
            barrier,
            inc=1,
            device_id=(lax.rem(group + offset, groups), me),
            device_id_type=MESH,
        )

    down = lax.broadcasted_iota(jnp.int32, (width, width), 0)
    right = lax.broadcasted_iota(jnp.int32, (width, width), 1)
    down_f, right_f = down.astype(jnp.float32), right.astype(jnp.float32)

    group_base = (group * (owners * pairs)).astype(jnp.float32)
    device_base = group_base + (me * pairs).astype(jnp.float32)

    def owner_and_slot(pair):
        at = pair.astype(jnp.float32) - group_base
        owner = jnp.floor((at + 0.5) / pairs)
        return owner, at - owner * pairs

    table[0:owners, :] = jnp.full((owners, width), -1.0, jnp.float32)
    table[owners:, :] = jnp.zeros((table.shape[0] - owners, width), jnp.float32)
    table[at_partner : at_partner + 1, :] = jnp.full((1, width), -1.0, jnp.float32)
    dst_owner, dst_slot = owner_and_slot(edge_dst[...])
    for o in range(owners):
        span = slice(o * edge_count, (o + 1) * edge_count)
        table[o : o + 1, 0:edge_count] = dst_owner[:, span]
        table[at_slot + o : at_slot + o + 1, 0:edge_count] = dst_slot[:, span]
    table[at_src : at_src + 1, 0:edge_count] = edge_src[...].astype(jnp.float32) - device_base
    table[at_fock : at_fock + 1, 0:edge_count] = edge_fock[...]
    partner, spot = owner_and_slot(mirror[...])
    table[at_partner : at_partner + 1, 0:pairs] = partner
    table[at_place : at_place + 1, 0:pairs] = spot
    for r in range(occ_rows):
        count = min(LANES, occ_count - r * LANES)
        table[at_occ + r : at_occ + r + 1, 0:count] = occ_energy[:, r * LANES : r * LANES + count]

    def along(row):
        return jnp.broadcast_to(table[pl.ds(row, 1), :], (width, width))

    def count_down(mask):
        return jnp.sum(jnp.where(mask, 1.0, 0.0), axis=0, keepdims=True)

    def count_right(mask):
        return jnp.sum(jnp.where(mask, 1.0, 0.0), axis=1, keepdims=True)

    def pick_down(mask, values):
        return jnp.sum(jnp.where(mask, values, 0.0), axis=0, keepdims=True)

    to_right = along(me)
    to_down = to_right.T
    nth = count_right((to_down == to_right) & (right < down))
    fills = (to_down * edge_cap + nth == right_f) & (to_down >= 0.0)
    early_rows[0:1, :] = pick_down(fills, down_f).astype(jnp.int32)
    early_rows[1:2, :] = pick_down(fills, along(at_src).T).astype(jnp.int32)
    early_rows[2:8, :] = jnp.zeros((6, width), jnp.int32)
    early_scale_rows[...] = jnp.broadcast_to(pick_down(fills, along(at_fock).T), (8, width))
    to_early = pltpu.make_async_copy(early_rows, early, table_sem.at[0])
    to_early_scales = pltpu.make_async_copy(early_scale_rows, early_scales, table_sem.at[1])
    to_early.start()
    to_early_scales.start()
    to_early.wait()
    to_early_scales.wait()

    pl.semaphore_wait(barrier, owners + groups - 2)

    def edge_copy(offset):
        target = lax.rem(me + offset, owners)
        return pltpu.make_async_remote_copy(
            src_ref=send_edge.at[pl.ds(target * edge_cap, edge_cap)],
            dst_ref=recv_edge.at[pl.ds(me * edge_cap, edge_cap)],
            send_sem=edge_send_sem.at[offset],
            recv_sem=edge_recv_sem.at[offset],
            device_id=(group, target),
            device_id_type=MESH,
        )

    def half_copy(offset):
        target = lax.rem(me + offset, owners)
        return pltpu.make_async_remote_copy(
            src_ref=send_half.at[pl.ds(target * mirror_cap, mirror_cap)],
            dst_ref=recv_half.at[pl.ds(me * mirror_cap, mirror_cap)],
            send_sem=half_send_sem.at[offset],
            recv_sem=half_recv_sem.at[offset],
            device_id=(group, target),
            device_id_type=MESH,
        )

    def grp_copy(offset):
        return pltpu.make_async_remote_copy(
            src_ref=grp_sums.at[group],
            dst_ref=grp_sums.at[group],
            send_sem=grp_send_sem.at[offset],
            recv_sem=grp_recv_sem.at[offset],
            device_id=(lax.rem(group + offset, groups), me),
            device_id_type=MESH,
        )

    def own_copy(offset):
        return pltpu.make_async_remote_copy(
            src_ref=own_sums.at[me],
            dst_ref=own_sums.at[me],
            send_sem=own_send_sem.at[offset],
            recv_sem=own_recv_sem.at[offset],
            device_id=(group, lax.rem(me + offset, owners)),
            device_id_type=MESH,
        )

    def send_step(step):
        offset = step_offset(step, owners)
        target = lax.rem(me + offset, owners)
        for k in range(edge_cap):
            slot = target * edge_cap + k
            tile = margin[within(early[0, slot], margin.shape[0])]
            projected = jnp.dot(
                tile, amps[within(early[1, slot], pairs)], preferred_element_type=jnp.float32
            ).astype(jnp.bfloat16)
            product = lax.dot_general(
                projected, tile, (((1,), (1,)), ((), ())), preferred_element_type=jnp.float32
            )
            send_edge[slot] = (product * early_scales[0, slot]).astype(jnp.bfloat16)
        edge_copy(offset).start()

    first = min(EARLY_STEPS, owners - 1)
    pl.loop(0, first)(send_step)

    rows = lax.broadcasted_iota(jnp.int32, (rank, rank), 0)
    columns = lax.broadcasted_iota(jnp.int32, (rank, rank), 1)
    on_diagonal = rows == columns
    occ_ids = lax.broadcasted_iota(
        jnp.int32, (occ_rows, LANES), 0
    ) * LANES + lax.broadcasted_iota(jnp.int32, (occ_rows, LANES), 1)

    def add_energy(p, partial):
        int_tile, amp_tile = ints[p], amps[p]
        product = jnp.dot(int_tile, amp_tile, preferred_element_type=jnp.float32)
        direct = 2.0 * int_tile.astype(jnp.float32) * amp_tile.astype(jnp.float32)
        terms = direct - jnp.where(on_diagonal, product, 0.0)
        energy = jnp.sum(jnp.sum(terms, axis=0, keepdims=True), axis=1, keepdims=True)
        return partial + jnp.where(occ_ids == occ[0, p], energy, 0.0)

    partial = lax.fori_loop(0, pairs, add_energy, jnp.zeros((occ_rows, LANES), jnp.float32))
    grp_sums[group] = partial

    @pl.loop(1, groups)
    def _(offset):
        grp_copy(offset).start()

    pl.loop(first, owners - 1)(send_step)

    @pl.loop(1, groups)
    def _(offset):
        grp_copy(offset).wait()

    own_sums[me] = jnp.sum(grp_sums[...], axis=0)

    @pl.loop(1, owners)
    def _(offset):
        own_copy(offset).start()

    for k in range(edge_cap):
        recv_edge[me * edge_cap + k] = jnp.zeros((rank, rank), jnp.bfloat16)

    arriving = table[0:owners, :] == me.astype(jnp.float32)
    before = jnp.dot(
        jnp.where(arriving, 1.0, 0.0).astype(jnp.bfloat16),
        jnp.where(down < right, 1.0, 0.0).astype(jnp.bfloat16),
        preferred_element_type=jnp.float32,
    )
    ends = table[at_slot : at_slot + owners, :] - pairs
    blocks = [
        jnp.broadcast_to(
            jnp.sum(jnp.where(arriving & (before == k), ends, 0.0), axis=1, keepdims=True) + pairs,
            (owners, width),
        )
        for k in range(edge_cap)
    ]
    if width > edge_slots:
        blocks.append(jnp.full((width - edge_slots, width), pairs, jnp.float32))
    end_down = jnp.concatenate(blocks, axis=0)
    end_right = end_down.T
    place = count_right((end_right < end_down) | ((end_right == end_down) & (right < down)))
    sender = lax.rem(down, owners)
    slot_down = (sender * edge_cap + lax.div(down, owners)).astype(jnp.float32)
    at_place_now = place == right_f
    order = pick_down(at_place_now, slot_down)
    sorted_end = pick_down(at_place_now, end_down)
    previous_end = pick_down(place + 1.0 == right_f, end_down)
    last = jnp.maximum(count_down(end_down <= right_f) - 1.0, 0.0)

    partner_right = along(at_partner)
    partner_down = partner_right.T
    spot_right = along(at_place)
    same = (partner_right == partner_down) & (partner_right >= 0.0)
    out_place = partner_right * mirror_cap + count_down(same & (down < right))
    in_place = partner_right * mirror_cap + count_down(same & (spot_right.T < spot_right))
    out_down = partner_down * mirror_cap + count_right(same & (right < down))
    packed = pick_down((out_down == right_f) & (partner_down >= 0.0), down_f)

    for row, values in enumerate(
        (order, last, packed, jnp.maximum(in_place[0:1], 0.0), jnp.maximum(out_place[0:1], 0.0))
    ):
        late_rows[row : row + 1, :] = values.astype(jnp.int32)
    late_rows[5:8, :] = jnp.zeros((3, width), jnp.int32)
    late_scale_rows[0:1, :] = jnp.where(sorted_end == previous_end, 1.0, 0.0)
    late_scale_rows[1:2, :] = jnp.minimum(count_down(end_down == right_f), 1.0)
    late_scale_rows[2:8, :] = jnp.zeros((6, width), jnp.float32)
    to_late = pltpu.make_async_copy(late_rows, late, table_sem.at[2])
    to_late_scales = pltpu.make_async_copy(late_scale_rows, late_scales, table_sem.at[3])
    to_late.start()
    to_late_scales.start()
    to_late.wait()
    to_late_scales.wait()

    @pl.loop(1, owners)
    def _(offset):
        own_copy(offset).wait()

    occ_terms = table[at_occ : at_occ + occ_rows, :LANES] + 0.5 * jnp.sum(own_sums[...], axis=0)

    @pl.loop(0, pairs)
    def _(p):
        hits = jnp.where(occ_ids == occ[0, p], occ_terms, 0.0) + jnp.where(
            occ_ids == occ[1, p], occ_terms, 0.0
        )
        shift = jnp.sum(jnp.sum(hits, axis=0, keepdims=True), axis=1, keepdims=True)
        across = jnp.broadcast_to(pno[pl.ds(p, 1), :], (rank, rank))
        diagonal = (across + across.T) - shift
        local_part[p] = 0.5 * ints[p].astype(jnp.float32) + diagonal * amps[p].astype(jnp.float32)

    @pl.loop(1, owners)
    def _(offset):
        edge_copy(offset).wait()

    def accumulate(j, total):
        total = total * late_scales[0, j] + recv_edge[within(late[0, j], edge_slots)].astype(jnp.float32)
        running[j] = total
        return total

    lax.fori_loop(0, edge_slots, accumulate, jnp.zeros((rank, rank), jnp.float32))

    @pl.loop(0, owners - 1)
    def _(step):
        offset = step_offset(step, owners)
        target = lax.rem(me + offset, owners)
        for k in range(mirror_cap):
            slot = target * mirror_cap + k
            p = within(late[2, slot], pairs)
            coupling = running[within(late[1, p], edge_slots)] * late_scales[1, p]
            send_half[slot] = (local_part[p] + coupling).astype(jnp.bfloat16)
        half_copy(offset).start()

    @pl.loop(0, owners - 1)
    def _(step):
        offset = step_offset(step, owners)
        half_copy(offset).wait_recv()
        sender = lax.rem(me - offset + owners, owners)
        for k in range(mirror_cap):
            slot = sender * mirror_cap + k
            flipped[slot] = recv_half[slot].astype(jnp.float32).T

    @pl.loop(0, pairs)
    def _(p):
        own_tile = send_half[within(late[4, p], half_slots)].astype(jnp.float32)
        out[p] = (own_tile + flipped[within(late[3, p], half_slots)]).astype(jnp.bfloat16)

    @pl.loop(1, owners)
    def _(offset):
        half_copy(offset).wait_send()


def local(
    amps, ints, pno_energy, occ_energy, pair_occ, mirror, edge_src, edge_dst, edge_fock, margin
):
    groups = lax.axis_size("grp")
    owners = lax.axis_size("own")
    pairs = amps.shape[0]
    rank = amps.shape[1]
    edge_count = edge_src.shape[0]
    occ_count = occ_energy.shape[0]
    mirror_cap = (pairs + owners - 2) // (owners - 1)
    edge_cap = (edge_count + owners - 2) // (owners - 1)
    edge_slots = owners * edge_cap
    half_slots = owners * mirror_cap
    occ_rows = -(-occ_count // LANES)
    widest = max(edge_count, edge_slots, half_slots, pairs, rank)
    width = -(-widest // LANES) * LANES

    height = -(-(2 * owners + 4 + occ_rows) // 8) * 8
    dims = (groups, owners, pairs, edge_cap, mirror_cap, occ_rows)
    vmem = pl.BlockSpec(memory_space=pltpu.VMEM)
    smem = pl.BlockSpec(memory_space=pltpu.SMEM)
    dma = pltpu.SemaphoreType.DMA
    return pl.pallas_call(
        functools.partial(kernel, dims),
        out_shape=jax.ShapeDtypeStruct(amps.shape, jnp.bfloat16),
        in_specs=[smem] + [vmem] * 9,
        out_specs=vmem,
        scratch_shapes=[
            pltpu.VMEM((edge_slots, rank, rank), jnp.bfloat16),
            pltpu.VMEM((edge_slots, rank, rank), jnp.bfloat16),
            pltpu.VMEM((edge_slots, rank, rank), jnp.float32),
            pltpu.VMEM((pairs, rank, rank), jnp.float32),
            pltpu.VMEM((half_slots, rank, rank), jnp.bfloat16),
            pltpu.VMEM((half_slots, rank, rank), jnp.bfloat16),
            pltpu.VMEM((half_slots, rank, rank), jnp.float32),
            pltpu.VMEM((groups, occ_rows, LANES), jnp.float32),
            pltpu.VMEM((owners, occ_rows, LANES), jnp.float32),
            pltpu.VMEM((height, width), jnp.float32),
            pltpu.VMEM((8, width), jnp.int32),
            pltpu.VMEM((8, width), jnp.float32),
            pltpu.VMEM((8, width), jnp.int32),
            pltpu.VMEM((8, width), jnp.float32),
            pltpu.SMEM((8, width), jnp.int32),
            pltpu.SMEM((8, width), jnp.float32),
            pltpu.SMEM((8, width), jnp.int32),
            pltpu.SMEM((8, width), jnp.float32),
            dma((4,)),
            dma((owners,)),
            dma((owners,)),
            dma((owners,)),
            dma((owners,)),
            dma((groups,)),
            dma((groups,)),
            dma((owners,)),
            dma((owners,)),
        ],
        compiler_params=pltpu.CompilerParams(
            collective_id=0, has_side_effects=True, vmem_limit_bytes=56 * 1024 * 1024
        ),
    )(
        pair_occ,
        occ_energy[None, :],
        mirror[None, :],
        edge_src[None, :],
        edge_dst[None, :],
        edge_fock[None, :],
        pno_energy,
        amps,
        ints,
        margin,
    )


def solution(mesh):
    in_specs = (
        P(("grp", "own"), None, None),
        P(("grp", "own"), None, None),
        P(("grp", "own"), None),
        P(),
        P(None, ("grp", "own")),
        P(("grp", "own")),
        P(("grp", "own")),
        P("grp"),
        P(("grp", "own")),
        P(("grp", "own"), None, None),
    )
    out_specs = P(("grp", "own"), None, None)
    return jax.shard_map(local, mesh=mesh, in_specs=in_specs, out_specs=out_specs, check_vma=False)
```

time: 99.8 us -> 90.7 us (0.909)
  other arithmetic: 6.16 us -> 0 us
  local copies, waits for them, and re-layouts: 6.06 us -> 3.47 us
    reduce_sum x11 -> x0, other arithmetic: 3.11 us -> none  [the longest x1 0.89 us: local(): fock_pair = jnp.sum(occ_hit * occ_energy[None, :], axis=1)]
    concatenate x2 -> x0, local copies, waits for them, and re-layouts: 1.35 us -> none  [the longest x1 0.68 us: local(): jnp.concatenate([slot_edge, slot_src, order, last, pair_occ[0], pair_occ[...]
    reshape x1 -> x0, local copies, waits for them, and re-layouts: 1.33 us -> none  [local(): pno_energy.reshape(pairs, 1, rank)]
    broadcast_in_dim x0 -> x1, local copies, waits for them, and re-layouts: none -> 1.27 us  [local(): edge_dst[None, :]]
where the time goes in v2:
time: 90.7 us; the launch traced here: 90.5 us
  Pallas kernels  87 us (96%)
  local copies, waits for them, and re-layouts  3.47 us (4%)
    pallas_call x1, Pallas kernels, local(): pl.pallas_call(functools.partial(kernel, dims), out_shape=jax.ShapeDtypeS...  87 us
    unnamed x1, local copies, waits for them, and re-layouts  2.2 us

profile of v2, /device:TPU:0, one launch (start us, length us, event | category | flops | bytes accessed | tf_op | source)
XLA Modules:
  0.0 90.5 jit_solution(87730322391827478)
XLA Ops:
  0.0 1.3 %broadcast_in_dim.18.edge_dst = s32[1,768]{1,0:T(1,128)} reshape(s32[768]{0:T(1024)} %param.17) | data formatting | bytes 6144 | tf_op jit(solution)/shard_map/broadcast_in_dim | solution.py:428
  1.3 87.0 %shard_map.100 = bf16[28,128,128]{2,1,0:T(8,128)(2,1)} custom-call(s32[2,28]{1,0:T(2,128)} %occ.1, f32[1,1000]{1,0:T(1,128)} %bitcast.4, s32[1,28]{1,0:T(1,128)} %bitcast.5, s32[1,48]{1,0:T(1,128)} %bitcast.6, s32[1,768]{1,0:T(1,128)} %broadcast_in_dim.18.edge_dst, f32[1,48]{1,0:T(1,128)} %bitcast.7, f32[28,128]{1,0:T(8,128)} %pno.1, ...), custom_call_target="tpu_custom_call" | custom-call | tf_op jit(solution)/shard_map/pallas_call | solution.py:386
  88.3 2.2 %copy.12 = bf16[28,128,128]{2,1,0:T(8,128)(2,1)} copy(bf16[28,128,128]{2,1,0:T(8,128)(2,1)} %shard_map.100) | data formatting | bytes 1835008
